TPU v7x, 32 devices: a whole 2x2x4 slice. The times are simulated.
32 devices in a mesh: grid: 16 (over z, x, core), col: 2 (over y).
Axes of the slice: x: 2, y: 2, z: 4, core: 2. Of those that a mesh axis runs over, the one named last changes fastest.
Arguments:
- density: bfloat16 [16384, 16384], P('grid', 'col'), may hold values from -0.5 to 0.5
- centres: float32 [3, 16384], replicated, may hold values from -0.4 to 0.4
- exponents: float32 [16384], replicated, may hold values from 2 to 16
- coords: float32 [64, 3, 256], P('grid'), may hold values from -0.4 to 0.4
- weights: float32 [64, 256], P('grid'), may hold values from 0.078125 to 0.78125
- core_density: float32 [64, 256], P('grid'), may hold values from 0.3 to 3
- counts: int32 [64], P('grid'), may hold values from 1 to 256, 4096 in all
- blocks: int32 [64, 2], replicated, may hold values from 0 to 127, as said below
Outputs:
- potential_matrix_xc: float32 [16384, 16384], P('grid', 'col')
- orbital_charge_samples: float32 [64, 256], P('grid')
- xc_batch_amounts: float32 [64], P('grid')
Inputs may be any that keep to these rules, and one draw needn't show every extreme that they name: Entry c of a batch's row names a block in the c-th of 2 equal runs of 64 blocks; for one grid index's 4 batches the values // 8 in one column c are distinct. The points in use are the first counts[b] slots.
All inputs are finite; a program needn't handle non-finite values. No bound on the sum of `counts` on one device may be relied on, other than what follows from the above.
Results may differ from a plain program's by a relative error of at most 0.0028.
Values may be sent and summed in bfloat16 or wider, within the bound.
A program may use at most 128 MiB of HBM per device.

v0:
```python
from functools import partial
import math

import jax
import jax.numpy as jnp
from jax import lax
from jax.sharding import PartitionSpec as P

BLK = 128
NB = 4
SUB = 128


kappa_pbe = 0.804
mu_coef = 0.2195
slater = -0.7385587663820224
grad_scale = 4.0 * (3.0 * math.pi**2) ** (2.0 / 3.0)
soft_square = 0.25


def pbe_energy(total, grad_square):
    regular = 0.5 * (total + jnp.sqrt(total * total + soft_square))
    scaled = grad_scale * jnp.power(regular, 8.0 / 3.0)
    enhance = (
        1.0
        + kappa_pbe
        - kappa_pbe * kappa_pbe * scaled / (kappa_pbe * scaled + mu_coef * grad_square)
    )
    return slater * jnp.power(regular, 4.0 / 3.0) * enhance


def xc_kernel(total, grad_square):
    total_functional_sum, pullback = jax.vjp(pbe_energy, total, grad_square)
    charge_derivative, deriv_sigma = pullback(jnp.ones_like(total_functional_sum))
    return (total_functional_sum, charge_derivative, deriv_sigma)


def basis(points, centre_rows, rate_rows):
    offset = points[:, :, None] - centre_rows[:, None, :]
    distance = jnp.sum(offset * offset, axis=0)
    value_entries = jnp.exp(-rate_rows[None, :] * distance)
    slopes = -2.0 * rate_rows[None, None, :] * offset * value_entries[None]
    return (value_entries, slopes)


def first_pass(batch_points, centre_rows, rate_rows, tile_panel, column, block_step, buffer):
    first_row = block_step * SUB
    points = lax.dynamic_slice_in_dim(batch_points, first_row, SUB, 1)
    value_entries, slopes = basis(points, centre_rows, rate_rows)
    values_low = value_entries.astype(jnp.bfloat16)
    own_low = lax.dynamic_slice_in_dim(values_low, column * BLK, BLK, 1)
    own_values = lax.dynamic_slice_in_dim(value_entries, column * BLK, BLK, 1)
    own_slopes = lax.dynamic_slice_in_dim(slopes, column * BLK, BLK, 2)
    right_sum = jnp.dot(values_low, tile_panel, preferred_element_type=jnp.float32)
    left_sum = lax.dot_general(
        own_low, tile_panel, (((1,), (1,)), ((), ())), preferred_element_type=jnp.float32
    )
    density_part = jnp.sum(own_values * right_sum, axis=1)
    gradient_part = jnp.sum(slopes * left_sum[None], axis=2) + jnp.sum(
        own_slopes * right_sum[None], axis=2
    )
    sub_piece = jnp.concatenate([density_part[None], gradient_part], axis=0)
    return lax.dynamic_update_slice_in_dim(buffer, sub_piece, first_row, 1)


def second_pass(
    batch_points, centre_rows, rate_rows, fweight, hweight, column, block_step, total_tile
):
    first_row = block_step * SUB
    points = lax.dynamic_slice_in_dim(batch_points, first_row, SUB, 1)
    fweight_sub = lax.dynamic_slice_in_dim(fweight, first_row, SUB, 0)
    hweight_sub = lax.dynamic_slice_in_dim(hweight, first_row, SUB, 1)
    value_entries, slopes = basis(points, centre_rows, rate_rows)
    values_low = value_entries.astype(jnp.bfloat16)
    across = jnp.sum(hweight_sub[:, :, None] * slopes, axis=0)
    along = fweight_sub[:, None] * lax.dynamic_slice_in_dim(
        value_entries, column * BLK, BLK, 1
    ) + lax.dynamic_slice_in_dim(across, column * BLK, BLK, 1)
    own_low = lax.dynamic_slice_in_dim(values_low, column * BLK, BLK, 1)
    left_side = jnp.concatenate([values_low, across.astype(jnp.bfloat16)], axis=0)
    right_side = jnp.concatenate([along.astype(jnp.bfloat16), own_low], axis=0)
    return total_tile + lax.dot_general(
        left_side, right_side, (((0,), (0,)), ((), ())), preferred_element_type=jnp.float32
    )


def kernel_on(summed, live_mask, point_weights, core_density):
    valence = live_mask * summed[:, 0]
    gradient = live_mask[:, None] * summed[:, 1:]
    grad_square = jnp.sum(gradient * gradient, axis=1)
    total_functional_sum, charge_derivative, deriv_sigma = xc_kernel(
        valence + core_density, grad_square
    )
    point_scale = point_weights * live_mask
    fweight = point_scale * charge_derivative
    hweight = (2.0 * point_scale * deriv_sigma)[:, None] * gradient
    return jnp.concatenate(
        [
            fweight[:, None],
            hweight,
            valence[:, None],
            (point_scale * total_functional_sum)[:, None],
        ],
        axis=1,
    )


def local(density, centres, exponents, coords, weights, core_density, counts, blocks):
    grid_point_count = lax.axis_size("grid")
    column_count = lax.axis_size("col")
    grid_index = lax.axis_index("grid")
    column = lax.axis_index("col")
    row_blocks = density.shape[0] // BLK
    col_blocks = density.shape[1] // BLK
    owner_groups = grid_point_count // column_count
    span_width = column_count * BLK
    points_len = coords.shape[2]
    offsets = jnp.arange(BLK, dtype=jnp.int32)
    block_table = blocks.reshape(grid_point_count, NB, column_count)
    held_rows = lax.dynamic_index_in_dim(block_table, grid_index, 0, keepdims=False)
    asked_rows = lax.dynamic_index_in_dim(
        block_table, grid_index // owner_groups, 2, keepdims=False
    )
    asked_cols = lax.dynamic_index_in_dim(block_table, column, 2, keepdims=False)
    matched = asked_rows // row_blocks == grid_index
    local_tile = asked_rows % row_blocks * col_blocks + asked_cols - column * col_blocks
    tile_slot = jnp.sum(jnp.where(matched, local_tile, 0), axis=1)
    has_tile = jnp.any(matched, axis=1)
    tile_ids = jnp.arange(row_blocks * col_blocks, dtype=jnp.int32)
    onehot = jnp.where(
        has_tile[:, None] & (tile_slot[:, None] == tile_ids[None, :]), 1.0, 0.0
    ).astype(jnp.float32)
    local_tiles = (
        density.reshape(row_blocks, BLK, col_blocks, BLK)
        .transpose(0, 2, 1, 3)
        .reshape(row_blocks * col_blocks, BLK * BLK)
    )
    outgoing = jnp.where(
        has_tile[:, None], jnp.take(local_tiles, tile_slot, axis=0), jnp.zeros((), jnp.bfloat16)
    )
    incoming = lax.all_to_all(outgoing, "grid", split_axis=0, concat_axis=0, tiled=True)
    holder_ranks = (held_rows // row_blocks).reshape(-1)
    fetched = jnp.take(incoming, holder_ranks, axis=0).reshape(NB, span_width, BLK)
    live_mask = (jnp.arange(points_len, dtype=jnp.int32)[None, :] < counts[:, None]).astype(
        jnp.float32
    )
    centre_list = []
    rate_list = []
    accumulated_totals = []
    for batch_id in range(NB):
        func_index = (held_rows[batch_id][:, None] * BLK + offsets[None, :]).reshape(-1)
        centre_rows = jnp.take(centres, func_index, axis=1)
        rate_rows = jnp.take(exponents, func_index)
        centre_list.append(centre_rows)
        rate_list.append(rate_rows)
        completed_steps = (counts[batch_id] + SUB - 1) // SUB
        step_function = partial(
            first_pass, coords[batch_id], centre_rows, rate_rows, fetched[batch_id], column
        )
        accumulated_totals.append(
            lax.fori_loop(
                0, completed_steps, step_function, jnp.zeros((4, points_len), jnp.float32)
            )
        )
    stacked = jnp.stack(accumulated_totals, axis=0)
    summed = lax.psum(stacked, "col")
    results = kernel_on(summed, live_mask, weights, core_density)
    tile_list = []
    for batch_id in range(NB):
        completed_steps = (counts[batch_id] + SUB - 1) // SUB
        step_function = partial(
            second_pass,
            coords[batch_id],
            centre_list[batch_id],
            rate_list[batch_id],
            results[batch_id, 0],
            results[batch_id, 1:4],
            column,
        )
        block_result_value = lax.fori_loop(
            0, completed_steps, step_function, jnp.zeros((span_width, BLK), jnp.float32)
        )
        tile_list.append(block_result_value.reshape(column_count, BLK * BLK))
    sending = (
        jnp.zeros((grid_point_count, BLK * BLK), jnp.float32)
        .at[holder_ranks]
        .set(jnp.concatenate(tile_list, axis=0))
    )
    arrived = lax.all_to_all(sending, "grid", split_axis=0, concat_axis=0, tiled=True)
    gathered = lax.dot_general(
        onehot,
        arrived,
        (((0,), (0,)), ((), ())),
        precision=lax.Precision.HIGHEST,
        preferred_element_type=jnp.float32,
    )
    potential_matrix_xc = (
        gathered.reshape(row_blocks, col_blocks, BLK, BLK)
        .transpose(0, 2, 1, 3)
        .reshape(row_blocks * BLK, col_blocks * BLK)
    )
    orbital_charge_samples = results[:, 4]
    xc_batch_amounts = jnp.sum(results[:, 5], axis=1)
    return (potential_matrix_xc, orbital_charge_samples, xc_batch_amounts)


def solution(mesh):
    return jax.shard_map(
        local,
        mesh=mesh,
        in_specs=(
            P("grid", "col"),
            P(),
            P(),
            P("grid", None, None),
            P("grid", None),
            P("grid", None),
            P("grid"),
            P(),
        ),
        out_specs=(P("grid", "col"), P("grid", None), P("grid")),
        check_vma=False,
    )
```

profile of v0, /device:TPU:0, one launch (start us, length us, event | category | flops | bytes accessed | tf_op | source)
XLA Modules:
  0.0 234.6 jit_solution(8201214514340330418)
XLA Ops:
  0.7 0.8 reshape.613
  1.7 9.7 %copy.179 = bf16[128,8,64,128]{3,2,1,0:T(8,128)(2,1)S(1)} copy(bf16[128,8,64,128]{3,1,2,0:T(8,128)(2,1)} %bitcast.206) | data formatting | bytes 33554432
  11.4 36.7 %copy.150 = bf16[8,128,64,128]{3,1,2,0:T(8,128)(2,1)S(1)} copy(bf16[8,128,64,128]{3,2,1,0:T(8,128)(2,1)S(1)} %bitcast.203) | data formatting | bytes 33554432 | tf_op jit(solution)/shard_map/reshape | solution.py:134
  48.1 15.3 %copy.201 = bf16[64,8,128,128]{3,1,2,0:T(8,128)(2,1)} copy(bf16[64,8,128,128]{3,2,1,0:T(8,128)(2,1)S(1)} %bitcast.202) | data formatting | bytes 33554432
  63.3 9.3 %gather_fusion = bf16[16,16384]{1,0:T(8,128)(2,1)S(1)} fusion(bf16[512,16384]{1,0:T(8,128)(2,1)} %bitcast.205, s32[1024]{0:T(1024)S(1)} %pad_clamp_fusion.4), kind=kCustom, calls=%fused_computation.8 | custom fusion | bytes 1048640 | tf_op jit(solution)/shard_map/jit(_take)/gather | solution.py:139
  72.7 0.5 broadcast.741
  73.3 1.0 reduce.8
  74.3 1.2 reshape.741
  75.5 7.4 %all-to-all-start = ((bf16[16,2,8192]{2,1,0:T(2,128)(2,1)}), bf16[16,2,8192]{2,1,0:T(2,128)(2,1)S(1)}, u32[]{:S(2)}, u32[]{:S(2)}) async-start(bf16[16,2,8192]{2,1,0:T(2,128)(2,1)} %reshape.741), calls=%async_computation | async-start | bytes 1048576 | tf_op jit(solution)/shard_map/all_to_all | solution.py:141
  82.8 0.6 fusion.132
  86.2 0.3 fusion.108
  86.6 1.7 gather_fusion.8
  88.4 1.7 gather_fusion.6
  90.1 5.1 %copy.148 = f32[3,16384]{0,1:T(8,128)} copy(f32[3,16384]{1,0:T(4,128)S(1)} %copy-done.2) | data formatting | bytes 393216 | tf_op args[1]
  95.2 4.1 %gather_fusion.9 = f32[256,3]{1,0:T(8,128)S(1)} fusion(f32[3,16384]{0,1:T(8,128)} %copy.148, s32[1024]{0:T(1024)S(1)} %pad_clamp_fusion), kind=kCustom, calls=%fused_computation.4.clone | custom fusion | bytes 7168 | tf_op jit(solution)/shard_map/jit(_take)/gather | solution.py:152
  99.3 4.1 %gather_fusion.7 = f32[256,3]{1,0:T(8,128)S(1)} fusion(f32[3,16384]{0,1:T(8,128)} %copy.148, s32[1024]{0:T(1024)S(1)} %pad_clamp_fusion.1), kind=kCustom, calls=%fused_computation.3.clone | custom fusion | bytes 7168 | tf_op jit(solution)/shard_map/jit(_take)/gather | solution.py:152
  103.4 1.7 gather_fusion.4
  105.2 4.1 %gather_fusion.5 = f32[256,3]{1,0:T(8,128)S(1)} fusion(f32[3,16384]{0,1:T(8,128)} %copy.148, s32[1024]{0:T(1024)S(1)} %pad_clamp_fusion.2), kind=kCustom, calls=%fused_computation.2.clone | custom fusion | bytes 7168 | tf_op jit(solution)/shard_map/jit(_take)/gather | solution.py:152
  109.3 1.7 gather_fusion.2
  111.0 4.1 %gather_fusion.3 = f32[256,3]{1,0:T(8,128)S(1)} fusion(f32[3,16384]{0,1:T(8,128)} %copy.148, s32[1024]{0:T(1024)S(1)} %pad_clamp_fusion.5), kind=kCustom, calls=%fused_computation.clone | custom fusion | bytes 7168 | tf_op jit(solution)/shard_map/jit(_take)/gather | solution.py:152
  116.2 0.5 reshape.742
  116.7 0.6 copy.202
  117.3 0.7 gather_fusion.1
  118.1 0.2 fusion.128
  118.4 1.5 while.96
  118.8 0.2 multiply_reduce_fusion.22
  119.3 0.2 fusion.203
  119.5 0.3 fusion.204
  119.7 0.1 multiply_reduce_fusion.23
  120.0 1.5 while.99
  120.4 0.2 multiply_reduce_fusion.28
  120.8 0.2 fusion.227
  121.0 0.3 fusion.228
  121.3 0.1 multiply_reduce_fusion.29
  121.6 1.5 while.98
  122.0 0.2 multiply_reduce_fusion.26
  122.4 0.2 fusion.219
  122.6 0.3 fusion.220
  122.9 0.1 multiply_reduce_fusion.27
  123.1 1.5 while.97
  123.5 0.2 multiply_reduce_fusion.24
  124.0 0.2 fusion.211
  124.2 0.3 fusion.212
  124.4 0.1 multiply_reduce_fusion.25
  124.7 8.2 %psum.7 = f32[4,4,256]{2,0,1:T(4,128)S(1)} all-reduce(f32[4,4,256]{2,0,1:T(4,128)S(1)} %pad_maximum_fusion), channel_id=1, replica_groups=mesh['grid'=16,'col'=2] {'col'}, use_global_device_ids=true, to_apply=%region_26.29 | all-reduce | flops 4096 | bytes 32768 | tf_op jit(solution)/shard_map/psum | solution.py:166
  132.9 0.7 multiply_reduce_fusion.13
  133.8 0.8 while.100
  134.1 0.2 fusion.233
  134.4 0.2 convolution_add_fusion.8
  134.8 0.8 while.103
  135.0 0.2 fusion.248
  135.3 0.2 convolution_add_fusion.11
  135.7 0.8 while.102
  136.0 0.2 fusion.243
  136.3 0.2 convolution_add_fusion.10
  136.6 0.8 while.101
  136.9 0.2 fusion.238
  137.2 0.2 convolution_add_fusion.9
  137.6 1.4 scatter_custom_fusion
  138.9 2.1 all_to_all.16
  141.0 9.6 %all-to-all-start.1 = ((f32[16,1,16384]{2,1,0:T(1,128)}), f32[16,1,16384]{2,1,0:T(1,128)S(1)}, u32[]{:S(2)}, u32[]{:S(2)}) async-start(f32[16,1,16384]{2,1,0:T(1,128)} %all_to_all.16), calls=%async_computation.1 | async-start | bytes 2097152 | tf_op jit(solution)/shard_map/all_to_all | solution.py:189
  150.6 22.9 %all-to-all-done.1 = f32[16,1,16384]{2,1,0:T(1,128)S(1)} async-done(((f32[16,1,16384]{2,1,0:T(1,128)}), f32[16,1,16384]{2,1,0:T(1,128)S(1)}, u32[]{:S(2)}, u32[]{:S(2)}) %all-to-all-start.1) | async-done | bytes 1048608 | tf_op jit(solution)/shard_map/all_to_all | solution.py:189
  173.5 27.2 %fusion.64 = f32[8,64,128,128]{3,1,2,0:T(8,128)S(1)} fusion(s32[8,64]{1,0:T(8,128)S(1)} %multiply_add_fusion.1, s32[16]{0:T(128)S(1)} %fusion.99, pred[16]{0:T(512)(128)(4,1)S(1)} %get-tuple-element.1468, f32[16,1,16384]{2,1,0:T(1,128)S(1)} %all-to-all-done.1), kind=kOutput, calls=%fused_computation.150 | convolution fusion | flops 1610637312 | bytes 34605136 | tf_op jit(solution)/shard_map/dot_general | solution.py:190
  200.7 33.9 %copy.200 = f32[128,8,64,128]{3,1,2,0:T(8,128)} copy(f32[128,8,64,128]{3,2,1,0:T(8,128)S(1)} %bitcast.201) | data formatting | bytes 67108864
  (155 shorter events, 6.2 us)
Async XLA Ops:
  0.6 86.0 %copy-start = (f32[16384]{0:T(1024)S(1)}, f32[16384]{0:T(1024)}, u32[]{:S(2)}) copy-start(f32[16384]{0:T(1024)} %param.30) | copy-start | bytes 196612
  48.0 34.8 %copy-start.3 = (s32[4]{0:T(128)S(1)}, s32[4]{0:T(128)}, u32[]{:S(2)}) copy-start(s32[4]{0:T(128)} %param.34) | copy-start | bytes 52
  48.0 42.0 %copy-start.2 = (f32[3,16384]{1,0:T(4,128)S(1)}, f32[3,16384]{1,0:T(4,128)}, u32[]{:S(2)}) copy-start(f32[3,16384]{1,0:T(4,128)} %param.29) | copy-start | bytes 589828
  63.3 52.8 %copy-start.7 = (f32[4,3,256]{2,0,1:T(4,128)S(1)}, f32[4,3,256]{2,0,1:T(4,128)}, u32[]{:S(2)}) copy-start(f32[4,3,256]{2,0,1:T(4,128)} %param.31) | copy-start | bytes 36868
  75.5 40.7 %all-to-all-start = ((bf16[16,2,8192]{2,1,0:T(2,128)(2,1)}), bf16[16,2,8192]{2,1,0:T(2,128)(2,1)S(1)}, u32[]{:S(2)}, u32[]{:S(2)}) async-start(bf16[16,2,8192]{2,1,0:T(2,128)(2,1)} %reshape.741), calls=%async_computation | async-start | bytes 1048576 | tf_op jit(solution)/shard_map/all_to_all | solution.py:141
  120.0 12.9 %copy-start.4 = (f32[4,256]{1,0:T(4,128)S(1)}, f32[4,256]{1,0:T(4,128)}, u32[]{:S(2)}) copy-start(f32[4,256]{1,0:T(4,128)} %param.32) | copy-start | bytes 12292
  120.0 12.9 %copy-start.5 = (f32[4,256]{1,0:T(4,128)S(1)}, f32[4,256]{1,0:T(4,128)}, u32[]{:S(2)}) copy-start(f32[4,256]{1,0:T(4,128)} %param.33) | copy-start | bytes 12292
  133.7 3.0 %copy-start.6 = (f32[4,256]{1,0:T(4,128)}, f32[4,256]{1,0:T(4,128)S(1)}, u32[]{:S(2)}) copy-start(f32[4,256]{1,0:T(4,128)S(1)} %get-tuple-element.1458) | copy-start | bytes 12292
  141.0 32.5 %all-to-all-start.1 = ((f32[16,1,16384]{2,1,0:T(1,128)}), f32[16,1,16384]{2,1,0:T(1,128)S(1)}, u32[]{:S(2)}, u32[]{:S(2)}) async-start(f32[16,1,16384]{2,1,0:T(1,128)} %all_to_all.16), calls=%async_computation.1 | async-start | bytes 2097152 | tf_op jit(solution)/shard_map/all_to_all | solution.py:189
  200.7 33.9 %copy-start.1 = (f32[16384]{0:T(1024)S(1)}, f32[16384]{0:T(1024)}, u32[]{:S(2)}) copy-start(f32[16384]{0:T(1024)} %param.30) | copy-start | bytes 196612
where the time goes:
time: 235 us
  local copies, waits for them, and re-layouts  143 us (61%)
  matrix products  29.9 us (13%)
  waiting for transfers between devices  22.9 us (10%)
  starting transfers between devices  17 us (7%)
  other arithmetic  8.87 us (4%)
  blocking collectives  8.25 us (4%)
  between operations  3.93 us (2%)
    unnamed x27, local copies, waits for them, and re-layouts  66.2 us
    reshape x1, local copies, waits for them, and re-layouts, local(): density.reshape(row_blocks, BLK, col_blocks, BLK).transpose(0, 2, 1, 3)  36.7 us
    dot_general x1, matrix products, local(): lax.dot_general(onehot, arrived, (((0,), (0,)), ((), ())), precision=lax....  27.2 us
    all_to_all x1, waiting for transfers between devices, local(): lax.all_to_all(sending, 'grid', split_axis=0, concat_axis=0, tiled=True)  22.9 us
    gather x4, local copies, waits for them, and re-layouts, local(): centre_rows = jnp.take(centres, func_index, axis=1)  16.4 us
    all_to_all x1, starting transfers between devices, local(): lax.all_to_all(sending, 'grid', split_axis=0, concat_axis=0, tiled=True)  9.6 us
    gather x1, local copies, waits for them, and re-layouts, local(): jnp.take(local_tiles, tile_slot, axis=0)  9.27 us
    psum x1, blocking collectives, local(): summed = lax.psum(stacked, 'col')  8.25 us
  transfers between devices with their start and end apart: 2, of which 1 were waited for; matrix products, arithmetic and copies ran while one was open for 13% of the time, Pallas kernels for 0%

commit v1 on v0

v1 whole, which is shorter than its diff:
```python
import math

import jax
import jax.numpy as jnp
from jax import lax
from jax.experimental import pallas as pl
from jax.experimental.pallas import tpu as pltpu
from jax.sharding import PartitionSpec as P

BLK = 128
FILL_ROWS = 32
FIRST_FILL = 0.5
VMEM_LIMIT = 48 * 1024 * 1024
MESH = pl.DeviceIdType.MESH
F32 = jnp.float32
BF16 = jnp.bfloat16

kappa_pbe = 0.804
mu_coef = 0.2195
slater = -0.7385587663820224
grad_scale = 4.0 * (3.0 * math.pi**2) ** (2.0 / 3.0)
soft_square = 0.25


def xc_kernel(total, grad_square):
    root = jnp.sqrt(total * total + soft_square)
    regular = 0.5 * (total + root)
    log_regular = jnp.log(regular)
    third = jnp.exp(log_regular * (1.0 / 3.0))
    four_thirds = jnp.exp(log_regular * (4.0 / 3.0))
    scaled = grad_scale * four_thirds * four_thirds
    inverse = 1.0 / (kappa_pbe * scaled + mu_coef * grad_square)
    ratio = scaled * inverse
    enhance = 1.0 + kappa_pbe - kappa_pbe * kappa_pbe * ratio
    energy = slater * four_thirds * enhance
    inner = (4.0 / 3.0) * enhance - (8.0 / 3.0) * kappa_pbe * kappa_pbe * ratio * (
        mu_coef * grad_square * inverse
    )
    deriv_density = slater * third * inner * (0.5 * (1.0 + total / root))
    deriv_sigma = slater * four_thirds * (kappa_pbe * kappa_pbe * mu_coef) * ratio * inverse
    return energy, deriv_density, deriv_sigma


def parts_of(value):
    first = value.astype(BF16).astype(F32)
    rest = value - first
    second = rest.astype(BF16).astype(F32)
    return first, second, rest - second


def outer_sum(left, right):
    l1, l2, l3 = parts_of(left)
    r1, r2, r3 = parts_of(right)
    lefts = jnp.concatenate([l1, l1, l1, l2, l2, l3], axis=0).astype(BF16)
    rights = jnp.concatenate([r1, r2, r3, r1, r2, r1], axis=0).astype(BF16)
    return lax.dot_general(
        lefts, rights, (((0,), (0,)), ((), ())), preferred_element_type=F32
    )


def batch_of(blocks_ref, requester, entry, owner, batches, row_blocks):
    found = jnp.int32(-1)
    for batch in range(batches):
        block = blocks_ref[requester * batches + batch, entry]
        found = jnp.where(lax.div(block, row_blocks) == owner, batch, found)
    return found


def exchange_points(sizes, blocks_ref, counts_ref, coords_ref, out_ref, staged, landed, send, recv):
    grid_size, col_size, batches, row_blocks, halves = sizes
    me, col = lax.axis_index("grid"), lax.axis_index("col")
    barrier = pltpu.get_barrier_semaphore()
    for step in range(1, grid_size):
        other = lax.rem(me + step, grid_size)
        pl.semaphore_signal(barrier, inc=1, device_id=(other, col), device_id_type=MESH)
    group = grid_size // col_size
    for owner in range(grid_size):
        batch = jnp.maximum(
            batch_of(blocks_ref, me, owner // group, owner, batches, row_blocks), 0
        )
        points = coords_ref[batch]
        count = jnp.full((1, BLK), counts_ref[batch].astype(F32), F32)
        pieces = []
        for half in range(halves):
            pieces += [points[:, half * BLK : (half + 1) * BLK], count]
        staged[owner] = jnp.concatenate(pieces, axis=0)
    pl.semaphore_wait(barrier, grid_size - 1)
    copies = []
    for step in range(1, grid_size):
        other = lax.rem(me + step, grid_size)
        copy = pltpu.make_async_remote_copy(
            src_ref=staged.at[other],
            dst_ref=landed.at[me],
            send_sem=send.at[step],
            recv_sem=recv.at[step],
            device_id=(other, col),
            device_id_type=MESH,
        )
        copy.start()
        copies.append(copy)
    landed[me] = staged[me]
    for copy in copies:
        copy.wait()
    out_ref[...] = landed[...]


def exchange_sums(
    sizes,
    blocks_ref,
    counts_ref,
    sums_ref,
    weights_ref,
    core_ref,
    out_ref,
    extra_ref,
    landed,
    col_sums,
    fields,
    staged,
    returned,
    send_a,
    recv_a,
    send_b,
    recv_b,
    send_c,
    recv_c,
):
    grid_size, col_size, batches, row_blocks, halves = sizes
    me, col = lax.axis_index("grid"), lax.axis_index("col")
    barrier = pltpu.get_barrier_semaphore()
    for step in range(1, grid_size):
        other = lax.rem(me + step, grid_size)
        pl.semaphore_signal(barrier, inc=1, device_id=(other, col), device_id_type=MESH)
    for step in range(1, col_size):
        other = lax.rem(col + step, col_size)
        pl.semaphore_signal(barrier, inc=1, device_id=(me, other), device_id_type=MESH)
    pl.semaphore_wait(barrier, grid_size + col_size - 2)

    copies = []
    for step in range(1, grid_size):
        other = lax.rem(me + step, grid_size)
        copy = pltpu.make_async_remote_copy(
            src_ref=sums_ref.at[other],
            dst_ref=landed.at[me],
            send_sem=send_a.at[step],
            recv_sem=recv_a.at[step],
            device_id=(other, col),
            device_id_type=MESH,
        )
        copy.start()
        copies.append(copy)
    landed[me] = sums_ref[me]
    for copy in copies:
        copy.wait()

    for batch in range(batches):
        total = None
        for entry in range(col_size):
            owner = lax.div(blocks_ref[me * batches + batch, entry], row_blocks)
            term = landed[owner]
            total = term if total is None else total + term
        col_sums[col, batch] = total
    copies = []
    for step in range(1, col_size):
        other = lax.rem(col + step, col_size)
        copy = pltpu.make_async_remote_copy(
            src_ref=col_sums.at[col],
            dst_ref=col_sums.at[col],
            send_sem=send_b.at[step],
            recv_sem=recv_b.at[step],
            device_id=(me, other),
            device_id_type=MESH,
        )
        copy.start()
        copies.append(copy)
    for copy in copies:
        copy.wait()
    summed = col_sums[0]
    for entry in range(1, col_size):
        summed = summed + col_sums[entry]

    places = [(batch, half) for batch in range(batches) for half in range(halves)]

    def rows_of(field):
        return jnp.concatenate(
            [summed[batch, 4 * half + field : 4 * half + field + 1] for batch, half in places],
            axis=0,
        )

    def rows_in(ref):
        value = ref[...]
        return jnp.concatenate(
            [value[batch : batch + 1, half * BLK : (half + 1) * BLK] for batch, half in places],
            axis=0,
        )

    lanes = lax.broadcasted_iota(jnp.int32, (1, BLK), 1)
    live = jnp.concatenate(
        [jnp.where(lanes + half * BLK < counts_ref[batch], 1.0, 0.0) for batch, half in places],
        axis=0,
    )
    valence = jnp.where(live > 0.0, rows_of(0), 0.0)
    gradient = [jnp.where(live > 0.0, rows_of(1 + d), 0.0) for d in range(3)]
    grad_square = (
        gradient[0] * gradient[0] + gradient[1] * gradient[1] + gradient[2] * gradient[2]
    )
    energy, deriv_density, deriv_sigma = xc_kernel(valence + rows_in(core_ref), grad_square)
    point_scale = rows_in(weights_ref) * live
    spread = 2.0 * point_scale * deriv_sigma
    table = [point_scale * deriv_density] + [spread * gradient[d] for d in range(3)]
    for batch in range(batches):
        fields[batch] = jnp.concatenate(
            [
                table[k][batch * halves + half : batch * halves + half + 1]
                for half in range(halves)
                for k in range(4)
            ],
            axis=0,
        )
    group = grid_size // col_size
    for owner in range(grid_size):
        batch = jnp.maximum(
            batch_of(blocks_ref, me, owner // group, owner, batches, row_blocks), 0
        )
        staged[owner] = fields[batch]
    copies = []
    for step in range(1, grid_size):
        other = lax.rem(me + step, grid_size)
        copy = pltpu.make_async_remote_copy(
            src_ref=staged.at[other],
            dst_ref=returned.at[me],
            send_sem=send_c.at[step],
            recv_sem=recv_c.at[step],
            device_id=(other, col),
            device_id_type=MESH,
        )
        copy.start()
        copies.append(copy)
    returned[me] = staged[me]
    extra_ref[0] = valence
    extra_ref[1] = point_scale * energy
    for copy in copies:
        copy.wait()
    out_ref[...] = returned[...]


def list_tiles(sizes, blocks_ref, points_ref, tile_slot, tile_row, tile_col, item_tile, item_half):
    grid_size, col_size, batches, row_blocks, halves = sizes
    me, col = lax.axis_index("grid"), lax.axis_index("col")
    entry = lax.div(me, grid_size // col_size)

    def step(slot, carry):
        tiles, items = carry
        found = batch_of(blocks_ref, slot, entry, me, batches, row_blocks)
        batch = jnp.maximum(found, 0)
        has = found >= 0
        tile_slot[tiles] = slot
        tile_row[tiles] = blocks_ref[slot * batches + batch, entry]
        tile_col[tiles] = blocks_ref[slot * batches + batch, col]
        count = points_ref[slot, 3, 0]
        for half in range(halves):
            item_tile[items] = tiles
            item_half[items] = half
            items = items + jnp.where(has & (count > half * BLK), 1, 0)
        return tiles + jnp.where(has, 1, 0), items

    return lax.fori_loop(0, grid_size, step, (jnp.int32(0), jnp.int32(0)))


def half_rows(value, half, halves):
    picked = value[0:4]
    for other in range(1, halves):
        picked = jnp.where(half == other, value[4 * other : 4 * other + 4], picked)
    return picked


def functions_of(centres_ref, exponents_ref, row, column):
    rate = jnp.concatenate(
        [exponents_ref[pl.ds(row, 1), :], exponents_ref[pl.ds(column, 1), :]], axis=1
    )
    centre = jnp.concatenate(
        [
            centres_ref[:, pl.ds(pl.multiple_of(row * BLK, BLK), BLK)],
            centres_ref[:, pl.ds(pl.multiple_of(column * BLK, BLK), BLK)],
        ],
        axis=1,
    )
    return rate, centre


def basis(points, rate, centre):
    square = jnp.sum(points * points, axis=0, keepdims=True)
    none = jnp.zeros((3, BLK), F32)
    right = jnp.concatenate([square, points, jnp.ones((1, BLK), F32), none], axis=0)
    left = jnp.concatenate(
        [
            -rate,
            2.0 * rate * centre,
            -rate * jnp.sum(centre * centre, axis=0, keepdims=True),
            jnp.zeros((3, 2 * BLK), F32),
        ],
        axis=0,
    )
    return jnp.exp(outer_sum(left, right))


def coefficients(rate, centre):
    lanes = lax.broadcasted_iota(jnp.int32, (1, 2 * BLK), 1)
    return jnp.concatenate(
        [
            rate,
            rate * centre,
            jnp.where(lanes >= BLK, 1.0, 0.0),
            jnp.zeros((3, 2 * BLK), F32),
        ],
        axis=0,
    )


def density_tiles(
    sizes,
    fills,
    blocks_ref,
    points_ref,
    density_ref,
    centres_ref,
    exponents_ref,
    sums_ref,
    matrix_ref,
    held,
    zeros,
    tile_slot,
    tile_row,
    tile_col,
    item_tile,
    item_half,
    tile_sem,
    fill_sem,
):
    grid_size, col_size, batches, row_blocks, halves = sizes
    col_blocks = density_ref.shape[1] // BLK
    first_row = lax.axis_index("grid") * row_blocks
    first_col = lax.axis_index("col") * col_blocks
    tiles, items = list_tiles(
        sizes, blocks_ref, points_ref, tile_slot, tile_row, tile_col, item_tile, item_half
    )

    def tile_copy(tile):
        row = pl.multiple_of((tile_row[tile] - first_row) * BLK, BLK)
        column = pl.multiple_of((tile_col[tile] - first_col) * BLK, BLK)
        return pltpu.make_async_copy(
            density_ref.at[pl.ds(row, BLK), pl.ds(column, BLK)], held.at[tile], tile_sem.at[tile]
        )

    def fill_copy(index):
        return pltpu.make_async_copy(
            zeros, matrix_ref.at[pl.ds(index * FILL_ROWS, FILL_ROWS), :], fill_sem.at[index]
        )

    @pl.loop(0, tiles)
    def _(tile):
        tile_copy(tile).start()

    zeros[...] = jnp.zeros_like(zeros)
    for index in range(fills):
        fill_copy(index).start()
    sums_ref[...] = jnp.zeros_like(sums_ref)

    @pl.loop(0, tiles)
    def _(tile):
        tile_copy(tile).wait()

    def one(item):
        tile, half = item_tile[item], item_half[item]
        slot = tile_slot[tile]
        points = half_rows(points_ref[slot], half, halves)[0:3]
        rate, centre = functions_of(centres_ref, exponents_ref, tile_row[tile], tile_col[tile])
        value = basis(points, rate, centre)
        low = value.astype(BF16)
        panel = held[tile]
        left_sum = jnp.dot(panel, low[BLK:], preferred_element_type=F32)
        right_sum = lax.dot_general(
            panel, low[:BLK], (((0,), (0,)), ((), ())), preferred_element_type=F32
        )
        product = value * jnp.concatenate([left_sum, right_sum], axis=0)
        summed = jnp.dot(
            coefficients(rate, centre),
            product,
            precision=lax.Precision.HIGHEST,
            preferred_element_type=F32,
        )
        gradient = 2.0 * (summed[1:4] - points * summed[0:1])
        piece = jnp.concatenate([summed[4:5], gradient], axis=0)
        rows = lax.broadcasted_iota(jnp.int32, (4 * halves, BLK), 0)
        return slot, (rows >= 4 * half) & (rows < 4 * half + 4), jnp.concatenate([piece] * halves, 0)

    @pl.loop(0, lax.div(items + 1, 2))
    def _(pair):
        results = [one(2 * pair), one(jnp.minimum(2 * pair + 1, items - 1))]
        for slot, chosen, piece in results:
            sums_ref[slot] = jnp.where(chosen, piece, sums_ref[slot])

    for index in range(fills):
        fill_copy(index).wait()


def potential_tiles(
    sizes,
    fills,
    blocks_ref,
    points_ref,
    fields_ref,
    extra_ref,
    centres_ref,
    exponents_ref,
    given_ref,
    matrix_ref,
    samples_ref,
    amounts_ref,
    total,
    zeros,
    tile_slot,
    tile_row,
    tile_col,
    item_tile,
    item_half,
    tile_goal,
    tile_sem,
    fill_sem,
):
    grid_size, col_size, batches, row_blocks, halves = sizes
    row_count, col_count = matrix_ref.shape
    first_row = lax.axis_index("grid") * row_blocks
    first_col = lax.axis_index("col") * (col_count // BLK)

    def fill_copy(index):
        return pltpu.make_async_copy(
            zeros, matrix_ref.at[pl.ds(index * FILL_ROWS, FILL_ROWS), :], fill_sem.at[index]
        )

    zeros[...] = jnp.zeros_like(zeros)
    every_fill = range(fills, row_count // FILL_ROWS)
    for index in every_fill:
        fill_copy(index).start()
    tiles, items = list_tiles(
        sizes, blocks_ref, points_ref, tile_slot, tile_row, tile_col, item_tile, item_half
    )
    total[...] = jnp.zeros_like(total)

    @pl.loop(0, tiles)
    def _(tile):
        def step(k, goal):
            other = tile - 1 - k
            same = (tile_row[other] == tile_row[tile]) & (tile_col[other] == tile_col[tile])
            return jnp.where(same, other, goal)

        tile_goal[tile] = lax.fori_loop(0, tile, step, tile)

    for batch in range(batches):
        for half in range(halves):
            place = batch * halves + half
            samples_ref[batch : batch + 1, half * BLK : (half + 1) * BLK] = extra_ref[
                0, place : place + 1, :
            ]
        amounts_ref[batch] = jnp.sum(extra_ref[1, batch * halves : (batch + 1) * halves, :])

    def one(item):
        tile, half = item_tile[item], item_half[item]
        slot = tile_slot[tile]
        points = half_rows(points_ref[slot], half, halves)[0:3]
        field = half_rows(fields_ref[slot], half, halves)
        rate, centre = functions_of(centres_ref, exponents_ref, tile_row[tile], tile_col[tile])
        value = basis(points, rate, centre)
        slant = -2.0 * jnp.sum(field[1:4] * points, axis=0, keepdims=True)
        right = jnp.concatenate(
            [slant, 2.0 * field[1:4], field[0:1], jnp.zeros((3, BLK), F32)], axis=0
        )
        weighted = (value * outer_sum(coefficients(rate, centre), right)).astype(BF16)
        low = value.astype(BF16)
        left_side = jnp.concatenate([low[:BLK], weighted[:BLK]], axis=1)
        right_side = jnp.concatenate([weighted[BLK:], low[BLK:]], axis=1)
        return tile, lax.dot_general(
            left_side, right_side, (((1,), (1,)), ((), ())), preferred_element_type=F32
        )

    @pl.loop(0, lax.div(items + 1, 2))
    def _(pair):
        tile_a, result_a = one(2 * pair)
        second = 2 * pair + 1
        tile_b, result_b = one(jnp.minimum(second, items - 1))
        goal_a = tile_goal[tile_a]
        goal_b = jnp.where(second < items, tile_goal[tile_b], grid_size)
        total[goal_a] += result_a
        total[goal_b] += result_b

    for index in every_fill:
        fill_copy(index).wait()

    def tile_copy(tile):
        row = pl.multiple_of((tile_row[tile] - first_row) * BLK, BLK)
        column = pl.multiple_of((tile_col[tile] - first_col) * BLK, BLK)
        return pltpu.make_async_copy(
            total.at[tile], matrix_ref.at[pl.ds(row, BLK), pl.ds(column, BLK)], tile_sem.at[tile]
        )

    @pl.loop(0, tiles)
    def _(tile):
        @pl.when(tile_goal[tile] == tile)
        def _():
            tile_copy(tile).start()

    @pl.loop(0, tiles)
    def _(tile):
        @pl.when(tile_goal[tile] == tile)
        def _():
            tile_copy(tile).wait()


def local(density, centres, exponents, coords, weights, core_density, counts, blocks):
    grid_size = lax.axis_size("grid")
    col_size = lax.axis_size("col")
    row_count, col_count = density.shape
    batches, _, points_len = coords.shape
    row_blocks = row_count // BLK
    halves = points_len // BLK
    sizes = (grid_size, col_size, batches, row_blocks, halves)
    rates = exponents.reshape(exponents.shape[0] // BLK, BLK)
    vmem = pl.BlockSpec(memory_space=pltpu.VMEM)
    smem = pl.BlockSpec(memory_space=pltpu.SMEM)
    anywhere = pl.BlockSpec(memory_space=pl.ANY)
    slot_shape = (grid_size, 4 * halves, BLK)
    slots = jax.ShapeDtypeStruct(slot_shape, F32)
    matrix = jax.ShapeDtypeStruct((row_count, col_count), F32)
    all_fills = row_count // FILL_ROWS
    fills = int(all_fills * FIRST_FILL)

    points = pl.pallas_call(
        lambda *refs: exchange_points(sizes, *refs),
        out_shape=slots,
        in_specs=[smem, smem, vmem],
        out_specs=vmem,
        scratch_shapes=[
            pltpu.VMEM(slot_shape, F32),
            pltpu.VMEM(slot_shape, F32),
            pltpu.SemaphoreType.DMA((grid_size,)),
            pltpu.SemaphoreType.DMA((grid_size,)),
        ],
        compiler_params=pltpu.CompilerParams(
            collective_id=0, has_side_effects=True, vmem_limit_bytes=VMEM_LIMIT
        ),
        name="exchange_points",
    )(blocks, counts, coords)

    lists = [pltpu.SMEM((grid_size + 1,), jnp.int32)] * 3 + [
        pltpu.SMEM((halves * grid_size + 1,), jnp.int32)
    ] * 2
    sums, started = pl.pallas_call(
        lambda *refs: density_tiles(sizes, fills, *refs),
        out_shape=(slots, matrix),
        in_specs=[smem, vmem, anywhere, vmem, vmem],
        out_specs=(vmem, anywhere),
        scratch_shapes=[
            pltpu.VMEM((grid_size, BLK, BLK), BF16),
            pltpu.VMEM((FILL_ROWS, col_count), F32),
            *lists,
            pltpu.SemaphoreType.DMA((grid_size,)),
            pltpu.SemaphoreType.DMA((all_fills,)),
        ],
        compiler_params=pltpu.CompilerParams(vmem_limit_bytes=VMEM_LIMIT),
        name="density_tiles",
    )(blocks, points, density, centres, rates)

    fields, extra = pl.pallas_call(
        lambda *refs: exchange_sums(sizes, *refs),
        out_shape=(slots, jax.ShapeDtypeStruct((2, batches * halves, BLK), F32)),
        in_specs=[smem, smem, vmem, vmem, vmem],
        out_specs=(vmem, vmem),
        scratch_shapes=[
            pltpu.VMEM(slot_shape, F32),
            pltpu.VMEM((col_size, batches, 4 * halves, BLK), F32),
            pltpu.VMEM((batches, 4 * halves, BLK), F32),
            pltpu.VMEM(slot_shape, F32),
            pltpu.VMEM(slot_shape, F32),
            pltpu.SemaphoreType.DMA((grid_size,)),
            pltpu.SemaphoreType.DMA((grid_size,)),
            pltpu.SemaphoreType.DMA((col_size,)),
            pltpu.SemaphoreType.DMA((col_size,)),
            pltpu.SemaphoreType.DMA((grid_size,)),
            pltpu.SemaphoreType.DMA((grid_size,)),
        ],
        compiler_params=pltpu.CompilerParams(
            collective_id=1, has_side_effects=True, vmem_limit_bytes=VMEM_LIMIT
        ),
        name="exchange_sums",
    )(blocks, counts, sums, weights, core_density)

    return pl.pallas_call(
        lambda *refs: potential_tiles(sizes, fills, *refs),
        out_shape=(
            matrix,
            jax.ShapeDtypeStruct((batches, points_len), F32),
            jax.ShapeDtypeStruct((batches,), F32),
        ),
        in_specs=[smem, vmem, vmem, vmem, vmem, vmem, anywhere],
        out_specs=(anywhere, vmem, smem),
        scratch_shapes=[
            pltpu.VMEM((grid_size + 1, BLK, BLK), F32),
            pltpu.VMEM((FILL_ROWS, col_count), F32),
            *lists,
            pltpu.SMEM((grid_size + 1,), jnp.int32),
            pltpu.SemaphoreType.DMA((grid_size,)),
            pltpu.SemaphoreType.DMA((all_fills,)),
        ],
        input_output_aliases={6: 0},
        compiler_params=pltpu.CompilerParams(vmem_limit_bytes=VMEM_LIMIT),
        name="potential_tiles",
    )(blocks, points, fields, extra, centres, rates, started)


def solution(mesh):
    return jax.shard_map(
        local,
        mesh=mesh,
        in_specs=(
            P("grid", "col"),
            P(),
            P(),
            P("grid", None, None),
            P("grid", None),
            P("grid", None),
            P("grid"),
            P(),
        ),
        out_specs=(P("grid", "col"), P("grid", None), P("grid")),
        check_vma=False,
    )
```

time: 235 us -> 53.3 us (0.23)
  local copies, waits for them, and re-layouts: 143 us -> 6.89 us
  Pallas kernels: 0 us -> 45.9 us
  matrix products: 29.9 us -> 0 us
  waiting for transfers between devices: 22.9 us -> 0 us
  starting transfers between devices: 17 us -> 0 us
  other arithmetic: 8.87 us -> 0 us
  blocking collectives: 8.25 us -> 0 us
  between operations: 3.93 us -> 0.68 us
    unnamed x27 -> x16, local copies, waits for them, and re-layouts: 66.2 us -> 6.89 us
    pallas_call x0 -> x4, Pallas kernels: none -> 45.9 us  [the longest x1 18.9 us: local(): pl.pallas_call(lambda *refs: exchange_sums(sizes, *refs), out_shape=(slot...]
    reshape x6 -> x0, local copies, waits for them, and re-layouts: 37.7 us -> none  [the longest x1 36.7 us: local(): density.reshape(row_blocks, BLK, col_blocks, BLK).transpose(0, 2, 1, 3)]
    gather x10 -> x0, local copies, waits for them, and re-layouts: 33.3 us -> none  [the longest x4 16.4 us: local(): centre_rows = jnp.take(centres, func_index, axis=1)]
    dot_general x13 -> x0, matrix products: 29.9 us -> none  [the longest x1 27.2 us: local(): lax.dot_general(onehot, arrived, (((0,), (0,)), ((), ())), precision=lax....]
    all_to_all x2 -> x0, waiting for transfers between devices: 22.9 us -> none  [the longest x1 22.9 us: local(): lax.all_to_all(sending, 'grid', split_axis=0, concat_axis=0, tiled=True)]
    all_to_all x2 -> x0, starting transfers between devices: 17 us -> none  [the longest x1 9.6 us: local(): lax.all_to_all(sending, 'grid', split_axis=0, concat_axis=0, tiled=True)]
    psum x1 -> x0, blocking collectives: 8.25 us -> none  [local(): summed = lax.psum(stacked, 'col')]
  transfers between devices with their start and end apart: 2 -> 0, of which waited for: 1 -> 0; matrix products, arithmetic and copies ran while one was open for 13% -> 0% of each run, Pallas kernels for 0% -> 0%
where the time goes in v1:
time: 53.3 us; the launch traced here: 53.5 us
  Pallas kernels  45.9 us (86%)
  local copies, waits for them, and re-layouts  6.89 us (13%)
  between operations  0.68 us (1%)
    pallas_call x1, Pallas kernels, local(): pl.pallas_call(lambda *refs: exchange_sums(sizes, *refs), out_shape=(slot...  18.9 us
    pallas_call x1, Pallas kernels, local(): pl.pallas_call(lambda *refs: exchange_points(sizes, *refs), out_shape=slo...  10 us
    pallas_call x1, Pallas kernels, local(): pl.pallas_call(lambda *refs: potential_tiles(sizes, fills, *refs), out_sh...  8.67 us
    pallas_call x1, Pallas kernels, local(): pl.pallas_call(lambda *refs: density_tiles(sizes, fills, *refs), out_shap...  8.34 us
    unnamed x16, local copies, waits for them, and re-layouts  6.89 us

profile of v1, /device:TPU:0, one launch (start us, length us, event | category | flops | bytes accessed | tf_op | source)
XLA Modules:
  0.0 53.5 jit_solution(7148711942169859284)
XLA Ops:
  0.6 0.7 %copy.13.refs_2_ = f32[4,3,256]{2,1,0:T(4,128)S(1)} copy(f32[4,3,256]{2,0,1:T(4,128)} %param.11) | data formatting | bytes 24576 | tf_op args[3]
  1.3 0.8 %copy.16.refs_0_ = s32[64,2]{1,0:T(8,128)S(1)} copy(s32[64,2]{0,1:T(2,128)} %param.15) | data formatting | bytes 1024 | tf_op args[7]
  2.1 0.0 copy-start.5
  2.1 0.7 %copy-done.5 = s32[4]{0:T(128)S(1)} copy-done((s32[4]{0:T(128)S(1)}, s32[4]{0:T(128)}, u32[]{:S(2)}) %copy-start.5) | copy-done | bytes 40
  2.8 10.0 %exchange_points.1.refs_1_ = f32[16,8,128]{2,1,0:T(8,128)S(1)} custom-call(s32[64,2]{1,0:T(8,128)S(1)} %copy.16.refs_0_, s32[4]{0:T(128)S(1)} %copy-done.5, f32[4,3,256]{2,1,0:T(4,128)S(1)} %copy.13.refs_2_), custom_call_target="tpu_custom_call" | custom-call | tf_op jit(solution)/shard_map/exchange_points/pallas_call | solution.py:537
  12.8 0.0 copy-start
  12.8 0.9 %copy-done = f32[3,16384]{1,0:T(4,128)S(1)} copy-done((f32[3,16384]{1,0:T(4,128)S(1)}, f32[3,16384]{1,0:T(4,128)}, u32[]{:S(2)}) %copy-start) | copy-done | bytes 196632
  13.7 0.0 copy-start.2
  13.8 0.8 %copy-done.2 = f32[16384]{0:T(1024)S(1)} copy-done((f32[16384]{0:T(1024)S(1)}, f32[16384]{0:T(1024)}, u32[]{:S(2)}) %copy-start.2) | copy-done | bytes 65560
  14.6 8.3 %density_tiles.1 = (f32[16,8,128]{2,1,0:T(8,128)S(1)}, f32[1024,8192]{1,0:T(8,128)}) custom-call(s32[64,2]{1,0:T(8,128)S(1)} %copy.16.refs_0_, f32[16,8,128]{2,1,0:T(8,128)S(1)} %exchange_points.1.refs_1_, bf16[1024,8192]{1,0:T(8,128)(2,1)} %refs_2_.2, f32[3,16384]{1,0:T(4,128)S(1)} %copy-done, f32[128,128]{1,0:T(8,128)S(1)} %bitcast.1), custom_call_target="tpu_custom_call" | custom-call | tf_op jit(solution)/shard_map/density_tiles/pallas_call | solution.py:557
  22.9 0.0 copy-start.3
  22.9 0.7 %copy-done.3 = f32[4,256]{1,0:T(4,128)S(1)} copy-done((f32[4,256]{1,0:T(4,128)S(1)}, f32[4,256]{1,0:T(4,128)}, u32[]{:S(2)}) %copy-start.3) | copy-done | bytes 4120
  23.6 0.0 copy-start.4
  23.6 0.7 %copy-done.4 = f32[4,256]{1,0:T(4,128)S(1)} copy-done((f32[4,256]{1,0:T(4,128)S(1)}, f32[4,256]{1,0:T(4,128)}, u32[]{:S(2)}) %copy-start.4) | copy-done | bytes 4120
  24.3 0.0 copy-start.6
  24.3 0.7 %copy-done.6 = s32[4]{0:T(128)S(1)} copy-done((s32[4]{0:T(128)S(1)}, s32[4]{0:T(128)}, u32[]{:S(2)}) %copy-start.6) | copy-done | bytes 40
  25.0 18.9 %exchange_sums.1 = (f32[16,8,128]{2,1,0:T(8,128)S(1)}, f32[2,8,128]{2,1,0:T(8,128)S(1)}) custom-call(s32[64,2]{1,0:T(8,128)S(1)} %copy.16.refs_0_, s32[4]{0:T(128)S(1)} %copy-done.6, f32[16,8,128]{2,1,0:T(8,128)S(1)} %get-tuple-element.7.refs_2_, f32[4,256]{1,0:T(4,128)S(1)} %copy-done.3, f32[4,256]{1,0:T(4,128)S(1)} %copy-done.4), custom_call_target="tpu_custom_call" | custom-call | tf_op jit(solution)/shard_map/exchange_sums/pallas_call | solution.py:573
  43.8 0.0 copy-start.1
  43.8 0.9 %copy-done.1 = f32[3,16384]{1,0:T(4,128)S(1)} copy-done((f32[3,16384]{1,0:T(4,128)S(1)}, f32[3,16384]{1,0:T(4,128)}, u32[]{:S(2)}) %copy-start.1) | copy-done | bytes 196632
  44.8 8.7 %potential_tiles.1 = (f32[1024,8192]{1,0:T(8,128)}, f32[4,256]{1,0:T(4,128)}, f32[4]{0:T(128)}) custom-call(s32[64,2]{1,0:T(8,128)S(1)} %copy.16.refs_0_, f32[16,8,128]{2,1,0:T(8,128)S(1)} %exchange_points.1.refs_1_, f32[16,8,128]{2,1,0:T(8,128)S(1)} %get-tuple-element.8.refs_2_, ...), custom_call_target="tpu_custom_call", output_to_operand_aliasing={{0}: (6, {})} | custom-call | tf_op jit(solution)/shard_map/potential_tiles/pallas_call | solution.py:597
Async XLA Ops:
  2.1 0.7 %copy-start.5 = (s32[4]{0:T(128)S(1)}, s32[4]{0:T(128)}, u32[]{:S(2)}) copy-start(s32[4]{0:T(128)} %refs_1_.3) | copy-start | bytes 52
  12.8 1.0 %copy-start = (f32[3,16384]{1,0:T(4,128)S(1)}, f32[3,16384]{1,0:T(4,128)}, u32[]{:S(2)}) copy-start(f32[3,16384]{1,0:T(4,128)} %refs_4_.3) | copy-start | bytes 589828
  13.7 0.8 %copy-start.2 = (f32[16384]{0:T(1024)S(1)}, f32[16384]{0:T(1024)}, u32[]{:S(2)}) copy-start(f32[16384]{0:T(1024)} %param.10) | copy-start | bytes 196612
  22.9 0.7 %copy-start.3 = (f32[4,256]{1,0:T(4,128)S(1)}, f32[4,256]{1,0:T(4,128)}, u32[]{:S(2)}) copy-start(f32[4,256]{1,0:T(4,128)} %refs_3_.3) | copy-start | bytes 12292
  23.6 0.7 %copy-start.4 = (f32[4,256]{1,0:T(4,128)S(1)}, f32[4,256]{1,0:T(4,128)}, u32[]{:S(2)}) copy-start(f32[4,256]{1,0:T(4,128)} %refs_4_.2) | copy-start | bytes 12292
  24.3 0.7 %copy-start.6 = (s32[4]{0:T(128)S(1)}, s32[4]{0:T(128)}, u32[]{:S(2)}) copy-start(s32[4]{0:T(128)} %refs_1_.3) | copy-start | bytes 52
  43.8 1.0 %copy-start.1 = (f32[3,16384]{1,0:T(4,128)S(1)}, f32[3,16384]{1,0:T(4,128)}, u32[]{:S(2)}) copy-start(f32[3,16384]{1,0:T(4,128)} %refs_4_.3) | copy-start | bytes 589828
